TPU v7x, 128 devices: a whole 4x4x4 slice. The times are simulated.
128 devices in a mesh: surf: 128 (over x, z, y, core).
Axes of the slice: x: 4, y: 4, z: 4, core: 2. Of those that a mesh axis runs over, the one named last changes fastest.
Arguments:
- signal: bfloat16 [16, 524288], P(None, 'surf'), may hold values from -6 to 6
- near_blocks: bfloat16 [2048, 8, 256, 256], P('surf'), may hold values from -0.375 to 0.375
- near_owner: int32 [2048, 8], P('surf'), may hold values from 0 to 127, as said below
- near_slot: int32 [2048, 8], P('surf'), may hold values from 0 to 15
- near_live: int32 [2048, 8], P('surf'), may hold values 0 or 1
- leaf_basis: bfloat16 [32, 524288], P(None, 'surf'), may hold values from -0.375 to 0.375
- transfer: float32 [2048, 1024], P('surf'), may hold values from -0.5 to 0.5
- leaf_coupling: float32 [2048, 32, 1024], P('surf'), may hold values from -0.1875 to 0.1875
- far_leaf: int32 [2048, 32], P('surf'), may hold values from 0 to 2047
- top_coupling: float32 [512, 32, 1024], P('surf'), may hold values from -0.1875 to 0.1875
- far_top: int32 [512, 32], P('surf'), may hold values from 0 to 511
Outputs:
- product: float32 [16, 524288], P(None, 'surf')
Inputs may be any that keep to these rules, and one draw needn't show every extreme that they name: `near_owner`: the owner of a neighbour is at most 4 positions away, counted cyclically along surf, from the device that holds cluster c; every device has pairs at distance 4 on both sides.
All inputs are finite; a program needn't handle non-finite values. No bound on the sum of `near_live` on one device may be relied on, other than what follows from the above.
Results may differ from a plain program's by a relative error of at most 0.0003.
Values may be sent and summed in bfloat16 or wider, within the bound.
A program may use at most 128 MiB of HBM per device.

v0:
```python
import jax
import jax.numpy as jnp
from jax import lax
from jax.sharding import PartitionSpec as P

HOPS = 4


exact_mode = lax.Precision.HIGHEST


def from_behind(block, axis, distance):
    devices = range(lax.axis_size(axis))
    route = [((i - distance) % len(devices), i) for i in devices]
    return lax.ppermute(block, axis, route)


def send_back(block, offset):
    return from_behind(block, "surf", offset)


def shards(
    signal,
    near_blocks,
    near_owner,
    near_slot,
    near_live,
    leaf_basis,
    transfer,
    leaf_coupling,
    far_leaf,
    top_coupling,
    far_top,
):
    rhs_count, local_panels = signal.shape
    rank_count = leaf_basis.shape[0]
    cluster_count, near_count = near_live.shape
    leaf_size = local_panels // cluster_count
    devices = lax.axis_size("surf")
    my_index = lax.axis_index("surf")
    entries = cluster_count * near_count
    window_count = 2 * HOPS + 1
    owner_ids = near_owner.reshape(entries)
    slot_ids = near_slot.reshape(entries)
    live_flags = near_live.reshape(entries)
    panel_rows = signal.reshape(rhs_count, cluster_count, leaf_size)
    offset_index = jnp.mod(owner_ids - my_index + HOPS, devices)
    window_id = offset_index * cluster_count + slot_ids
    pieces = [signal for position in range(window_count)]
    for distance in range(-HOPS, HOPS + 1):
        if distance != 0:
            pieces[distance + HOPS] = from_behind(signal, "surf", -distance)
    window = jnp.concatenate(pieces, axis=1)
    remote = jnp.take(
        window.reshape(rhs_count, window_count * cluster_count, leaf_size), window_id, axis=1
    )
    weight = live_flags.astype(jnp.float32)
    blocks = near_blocks.reshape(entries, leaf_size, leaf_size)
    own_rows = jnp.repeat(panel_rows, near_count, axis=1)
    near_inward = (
        jnp.einsum("qeb,eab->qea", remote, blocks, preferred_element_type=jnp.float32)
        * weight[None, :, None]
    )
    near_local = near_inward.reshape(rhs_count, cluster_count, near_count, leaf_size).sum(axis=2)
    outgoing = (
        jnp.einsum("qea,eab->qeb", own_rows, blocks, preferred_element_type=jnp.float32)
        * weight[None, :, None]
    )
    window_hot = (
        window_id[:, None] == jnp.arange(window_count * cluster_count, dtype=jnp.int32)[None, :]
    ).astype(jnp.float32)
    window_terms = jnp.einsum("qeb,ew->qwb", outgoing, window_hot, precision=exact_mode)
    near_back = window_terms[:, HOPS * cluster_count : (HOPS + 1) * cluster_count, :]
    for offset in range(-HOPS, HOPS + 1):
        if offset != 0:
            first = (offset + HOPS) * cluster_count
            near_back = near_back + send_back(
                window_terms[:, first : first + cluster_count, :], offset
            )
    shapes = leaf_basis.reshape(rank_count, cluster_count, leaf_size)
    moments = jnp.einsum(
        "rca,qca->crq", shapes, panel_rows, preferred_element_type=jnp.float32
    ).reshape(cluster_count, rank_count * rhs_count)
    far_count = far_leaf.shape[1]
    wanted = far_leaf.reshape(-1)
    piece = lax.all_gather(moments, "surf", axis=0, tiled=True)
    inside = (wanted >= 0) & (wanted < piece.shape[0])
    taken_rows = jnp.take(piece, jnp.clip(wanted, 0, piece.shape[0] - 1), axis=0)
    picked = jnp.where(
        inside[:, None],
        taken_rows,
        jnp.zeros((wanted.shape[0], rank_count * rhs_count), jnp.float32),
    )
    coupling = leaf_coupling.reshape(cluster_count, far_count, rank_count, rank_count)
    leaf_field = jnp.einsum(
        "ckrs,cksq->crq",
        coupling,
        picked.reshape(cluster_count, far_count, rank_count, rhs_count),
        precision=exact_mode,
    )
    parent_count = far_top.shape[0]
    branch = cluster_count // parent_count
    lift_maps = transfer.reshape(parent_count, branch, rank_count, rank_count)
    upper_moments = jnp.einsum(
        "pbrs,pbsq->prq",
        lift_maps,
        moments.reshape(parent_count, branch, rank_count, rhs_count),
        precision=exact_mode,
    )
    parent_table = lax.all_gather(
        upper_moments.reshape(parent_count, rank_count * rhs_count), "surf", axis=0, tiled=True
    )
    top_count = far_top.shape[1]
    chosen = jnp.take(parent_table, far_top.reshape(-1), axis=0).reshape(
        parent_count, top_count, rank_count, rhs_count
    )
    top_field = jnp.einsum(
        "pkrs,pksq->prq",
        top_coupling.reshape(parent_count, top_count, rank_count, rank_count),
        chosen,
        precision=exact_mode,
    )
    downward = jnp.einsum("pbrs,prq->pbsq", lift_maps, top_field, precision=exact_mode).reshape(
        cluster_count, rank_count, rhs_count
    )
    field = (leaf_field + downward).astype(jnp.bfloat16)
    far_part = jnp.einsum("crq,rca->qca", field, shapes, preferred_element_type=jnp.float32)
    combined = near_local + near_back + far_part
    return combined.reshape(rhs_count, local_panels)


def solution(mesh):
    placed = (
        P(None, "surf"),
        P("surf", None, None, None),
        P("surf", None),
        P("surf", None),
        P("surf", None),
        P(None, "surf"),
        P("surf", None),
        P("surf", None, None),
        P("surf", None),
        P("surf", None, None),
        P("surf", None),
    )
    return jax.shard_map(
        shards, mesh=mesh, in_specs=placed, out_specs=P(None, "surf"), check_vma=False
    )
```

profile of v0, /device:TPU:1, one launch (start us, length us, event | category | flops | bytes accessed | tf_op | source)
XLA Modules:
  0.0 203.2 jit_solution(15102741952741018569)
XLA Ops:
  10.1 3.8 %collective-permute-start = (bf16[16,4096]{1,0:T(8,128)(2,1)}, bf16[16,4096]{1,0:T(8,128)(2,1)}, u32[]{:S(2)}, u32[]{:S(2)}) collective-permute-start(bf16[16,4096]{1,0:T(8,128)(2,1)} %param.11), channel_id=1, source_target_pairs={{124,0},{125,1},{126,2},{127,3},{0,4},{1,5},{2,6},{3,7},{4,8},{5,9... | collective-permute-start | bytes 393224 | tf_op jit(solution)/shard_map/ppermute | solution.py:15
  13.9 2.3 %collective-permute-start.1 = (bf16[16,4096]{1,0:T(8,128)(2,1)}, bf16[16,4096]{1,0:T(8,128)(2,1)}, u32[]{:S(2)}, u32[]{:S(2)}) collective-permute-start(bf16[16,4096]{1,0:T(8,128)(2,1)} %param.11), channel_id=1, source_target_pairs={{125,0},{126,1},{127,2},{0,3},{1,4},{2,5},{3,6},{4,7},{5,8},{6,9},... | collective-permute-start | bytes 393224 | tf_op jit(solution)/shard_map/ppermute | solution.py:15
  21.1 8.1 %multiply_bitcast_fusion = f32[16,128,256]{2,0,1:T(8,128)S(1)} fusion(bf16[16,128,256]{2,0,1:T(8,128)(2,1)S(1)} %bitcast.83, bf16[128,256,256]{2,1,0:T(8,128)(2,1)} %bitcast.81, f32[128]{0:T(128)S(1)} %convert_element_type.15), kind=kOutput, calls=%fused_computation.7 | convolution fusion | flops 268959744 | bytes 19923456 | tf_op jit(solution)/shard_map/qea,eab->qeb/dot_general | solution.py:66
  29.2 2.5 %fusion.2 = f32[16,144,256]{2,1,0:T(8,128)S(1)} fusion(f32[16,128,256]{2,0,1:T(8,128)S(1)} %multiply_bitcast_fusion, s32[128]{0:T(128)S(1)} %get-tuple-element.6), kind=kOutput, calls=%fused_computation.8 | convolution fusion | flops 905988096 | bytes 4456960 | tf_op jit(solution)/shard_map/qeb,ew->qwb/dot_general | solution.py:72
  33.7 2.0 reshape.246
  35.7 6.5 %reshape.242 = f32[16,32,32,32]{3,2,1,0:T(8,128)} reshape(f32[16,32,1024]{2,1,0:T(8,128)} %param.18) | data formatting | bytes 4194304 | tf_op jit(solution)/shard_map/reshape | solution.py:94
  42.8 5.6 %collective-permute-start.5 = (bf16[16,4096]{1,0:T(8,128)(2,1)S(1)}, bf16[16,4096]{1,0:T(8,128)(2,1)S(1)}, u32[]{:S(2)}, u32[]{:S(2)}) collective-permute-start(bf16[16,4096]{1,0:T(8,128)(2,1)S(1)} %copy-done.4), channel_id=1, source_target_pairs={{2,0},{3,1},{4,2},{5,3},{6,4},{7,5},{8,6},{9,7},{10,8},{11,9},{12,... | collective-permute-start | bytes 393224 | tf_op jit(solution)/shard_map/ppermute | solution.py:15
  51.6 3.7 %collective-permute-start.7 = (bf16[16,4096]{1,0:T(8,128)(2,1)S(1)}, bf16[16,4096]{1,0:T(8,128)(2,1)S(1)}, u32[]{:S(2)}, u32[]{:S(2)}) collective-permute-start(bf16[16,4096]{1,0:T(8,128)(2,1)S(1)} %copy-done.4), channel_id=1, source_target_pairs={{4,0},{5,1},{6,2},{7,3},{8,4},{9,5},{10,6},{11,7},{12,8},{13,9},{1... | collective-permute-start | bytes 393224 | tf_op jit(solution)/shard_map/ppermute | solution.py:15
  57.2 2.0 collective-permute-start.12
  59.4 2.5 %collective-permute-start.14 = (f32[16,16,256]{2,1,0:T(8,128)}, f32[16,16,256]{2,1,0:T(8,128)}, u32[]{:S(2)}, u32[]{:S(2)}) collective-permute-start(f32[16,16,256]{2,1,0:T(8,128)} %get-tuple-element.9), channel_id=1, source_target_pairs={{125,0},{126,1},{127,2},{0,3},{1,4},{2,5},{3,6},{4,7},{5,8},{6,9},... | collective-permute-start | bytes 786440 | tf_op jit(solution)/shard_map/ppermute | solution.py:15
  63.1 2.0 %gather_fusion = bf16[128,16,256]{2,1,0:T(8,128)(2,1)S(1)} fusion(bf16[16,144,256]{2,0,1:T(8,128)(2,1)} %bitcast.84, s32[1024]{0:T(1024)} %pad_clamp_fusion.2), kind=kCustom, calls=%fused_computation | custom fusion | bytes 2097664 | tf_op jit(solution)/shard_map/jit(_take)/gather | solution.py:54
  65.1 11.0 %bitcast_reduce_fusion = f32[16,16,256]{2,0,1:T(8,128)} fusion(f32[128]{0:T(128)S(1)} %convert_element_type.15, bf16[128,256,256]{2,1,0:T(8,128)(2,1)} %bitcast.82, bf16[128,16,256]{2,1,0:T(8,128)(2,1)S(1)} %gather_fusion, pred[128]{0:T(512)(128)(4,1)S(1)} %copy-done.14), kind=kOutput, calls=%fused_computation.4 | convolution fusion | flops 269942784 | bytes 18088576 | tf_op jit(solution)/shard_map/qeb,eab->qea/dot_general | solution.py:61
  76.1 12.2 %all-gather.6.cloned.1.call-done = f32[128,4,512]{2,1,0:T(4,128)} async-done(((f32[1,4,512]{2,1,0:T(4,128)}), f32[128,4,512]{2,1,0:T(4,128)}) %all-gather.6.cloned.1.call-update) | async-done | bytes 1048592 | tf_op jit(solution)/shard_map/all_gather | solution.py:110
  91.5 1.8 copy.67
  95.9 2.0 copy.68
  97.9 3.6 %fusion.42 = f32[4,16,32,1]{2,1,3,0:T(8,128)S(1)} fusion(f32[4,32,32,16]{2,3,1,0:T(8,128)S(1)} %copy.68, f32[4,32,32,32]{3,2,1,0:T(8,128)} %reshape.246), kind=kOutput, calls=%fused_computation.80 | convolution fusion | flops 25165824 | bytes 794624 | tf_op jit(solution)/shard_map/pkrs,pksq->prq/dot_general | solution.py:117
  101.8 53.8 %all-gather.4.cloned.1.call-done = f32[2048,512]{1,0:T(8,128)} async-done(((f32[16,512]{1,0:T(8,128)}), f32[2048,512]{1,0:T(8,128)}) %all-gather.4.cloned.1.call-update) | async-done | bytes 4194320 | tf_op jit(solution)/shard_map/all_gather | solution.py:86
  155.6 4.2 %gather_fusion.1 = f32[512,512]{1,0:T(8,128)S(1)} fusion(f32[2048,512]{1,0:T(8,128)} %all-gather.4.cloned.1.call-done, s32[1024]{0:T(1024)S(1)} %pad_clamp_fusion.1), kind=kCustom, calls=%fused_computation.1 | custom fusion | bytes 2099200 | tf_op jit(solution)/shard_map/jit(_take)/gather | solution.py:88
  161.2 3.8 %gather.18 = f32[16,32,32,16]{1,0,3,2:T(8,128)} reshape(f32[512,512]{0,1:T(8,128)} %copy.64) | data formatting | bytes 2097152 | tf_op jit(solution)/shard_map/jit(_take)/gather | solution.py:88
  164.9 4.8 %select_select_fusion = f32[16,32,32,16]{1,0,3,2:T(8,128)} fusion(f32[16,32,32,16]{1,0,3,2:T(8,128)} %gather.18, pred[16,32]{1,0:T(8,128)(4,1)S(1)} %get-tuple-element.16, pred[16,32]{1,0:T(8,128)(4,1)S(1)} %get-tuple-element.15), kind=kLoop, calls=%fused_computation.3 | loop fusion | flops 524288 | bytes 2098176 | tf_op jit(solution)/shard_map/jit(_where)/select_n | solution.py:89
  169.7 6.0 %copy.65 = f32[16,32,32,16]{2,3,1,0:T(8,128)} copy(f32[16,32,32,16]{1,0,3,2:T(8,128)} %select_select_fusion) | data formatting | bytes 2097152 | tf_op jit(solution)/shard_map/jit(_where)/select_n | solution.py:89
  177.0 6.0 %collective-permute-start.8 = (f32[16,16,256]{2,1,0:T(8,128)S(1)}, f32[16,16,256]{2,1,0:T(8,128)S(1)}, u32[]{:S(2)}, u32[]{:S(2)}) collective-permute-start(f32[16,16,256]{2,1,0:T(8,128)S(1)} %copy-done.6), channel_id=1, source_target_pairs={{4,0},{5,1},{6,2},{7,3},{8,4},{9,5},{10,6},{11,7},{12,8},{13,9},{1... | collective-permute-start | bytes 786440 | tf_op jit(solution)/shard_map/ppermute | solution.py:15
  183.1 10.4 %fusion.6 = bf16[16,32,16]{1,2,0:T(8,128)(2,1)S(1)} fusion(f32[16,32,16]{1,2,0:T(8,128)S(1)} %bitcast.87, f32[16,32,32,16]{2,3,1,0:T(8,128)} %copy.65, f32[16,32,32,32]{3,2,1,0:T(8,128)} %reshape.242), kind=kOutput, calls=%fused_computation.13 | convolution fusion | flops 100679680 | bytes 3194880 | tf_op jit(solution)/shard_map/ckrs,cksq->crq/dot_general | solution.py:95
  193.7 1.8 fusion.25
  (111 shorter events, 27.0 us)
Async XLA Ops:
  6.5 13.7 %copy-start.4 = (bf16[16,4096]{1,0:T(8,128)(2,1)S(1)}, bf16[16,4096]{1,0:T(8,128)(2,1)}, u32[]{:S(2)}) copy-start(bf16[16,4096]{1,0:T(8,128)(2,1)} %param.11) | copy-start | bytes 393220
  6.5 12.9 %copy-start.9 = (s32[16,32]{1,0:T(8,128)S(1)}, s32[16,32]{1,0:T(8,128)}, u32[]{:S(2)}) copy-start(s32[16,32]{1,0:T(8,128)} %param.19) | copy-start | bytes 6148
  6.5 13.0 %copy-start.10 = (s32[4,32]{1,0:T(4,128)S(1)}, s32[4,32]{1,0:T(4,128)}, u32[]{:S(2)}) copy-start(s32[4,32]{1,0:T(4,128)} %param.21) | copy-start | bytes 1540
  6.5 13.7 %copy-start.13 = (s32[16,8]{0,1:T(8,128)S(1)}, s32[16,8]{0,1:T(8,128)}, u32[]{:S(2)}) copy-start(s32[16,8]{0,1:T(8,128)} %param.15) | copy-start | bytes 1540
  6.6 81.8 %all-gather.6.cloned.1.call-start = ((), (), s32[]{:S(2)}) async-start(), calls=%async_computation.1 | async-start | bytes 1056768 | tf_op jit(solution)/shard_map/all_gather | solution.py:110
  7.6 21.6 %copy-start = (f32[4,4,32,32]{3,2,1,0:T(8,128)}, f32[4,4,32,32]{3,2,1,0:T(8,128)S(1)}, u32[]{:S(2)}) copy-start(f32[4,4,32,32]{3,2,1,0:T(8,128)S(1)} %reshape.243) | copy-start | bytes 196612
  10.1 145.6 %all-gather.4.cloned.1.call-start = ((), (), s32[]{:S(2)}) async-start(), calls=%async_computation | async-start | bytes 4227072 | tf_op jit(solution)/shard_map/all_gather | solution.py:86
  10.1 32.7 %collective-permute-start = (bf16[16,4096]{1,0:T(8,128)(2,1)}, bf16[16,4096]{1,0:T(8,128)(2,1)}, u32[]{:S(2)}, u32[]{:S(2)}) collective-permute-start(bf16[16,4096]{1,0:T(8,128)(2,1)} %param.11), channel_id=1, source_target_pairs={{124,0},{125,1},{126,2},{127,3},{0,4},{1,5},{2,6},{3,7},{4,8},{5,9... | collective-permute-start | bytes 393224 | tf_op jit(solution)/shard_map/ppermute | solution.py:15
  13.9 35.4 %collective-permute-start.1 = (bf16[16,4096]{1,0:T(8,128)(2,1)}, bf16[16,4096]{1,0:T(8,128)(2,1)}, u32[]{:S(2)}, u32[]{:S(2)}) collective-permute-start(bf16[16,4096]{1,0:T(8,128)(2,1)} %param.11), channel_id=1, source_target_pairs={{125,0},{126,1},{127,2},{0,3},{1,4},{2,5},{3,6},{4,7},{5,8},{6,9},... | collective-permute-start | bytes 393224 | tf_op jit(solution)/shard_map/ppermute | solution.py:15
  16.2 35.4 %collective-permute-start.2 = (bf16[16,4096]{1,0:T(8,128)(2,1)}, bf16[16,4096]{1,0:T(8,128)(2,1)S(1)}, u32[]{:S(2)}, u32[]{:S(2)}) collective-permute-start(bf16[16,4096]{1,0:T(8,128)(2,1)} %param.11), channel_id=1, source_target_pairs={{126,0},{127,1},{0,2},{1,3},{2,4},{3,5},{4,6},{5,7},{6,8},{7,9},{8... | collective-permute-start | bytes 393224 | tf_op jit(solution)/shard_map/ppermute | solution.py:15
  17.5 37.9 %collective-permute-start.3 = (bf16[16,4096]{1,0:T(8,128)(2,1)}, bf16[16,4096]{1,0:T(8,128)(2,1)S(1)}, u32[]{:S(2)}, u32[]{:S(2)}) collective-permute-start(bf16[16,4096]{1,0:T(8,128)(2,1)} %param.11), channel_id=1, source_target_pairs={{127,0},{0,1},{1,2},{2,3},{3,4},{4,5},{5,6},{6,7},{7,8},{8,9},{9,1... | collective-permute-start | bytes 393224 | tf_op jit(solution)/shard_map/ppermute | solution.py:15
  17.5 39.6 %collective-permute-start.4 = (bf16[16,4096]{1,0:T(8,128)(2,1)}, bf16[16,4096]{1,0:T(8,128)(2,1)S(1)}, u32[]{:S(2)}, u32[]{:S(2)}) collective-permute-start(bf16[16,4096]{1,0:T(8,128)(2,1)} %param.11), channel_id=1, source_target_pairs={{1,0},{2,1},{3,2},{4,3},{5,4},{6,5},{7,6},{8,7},{9,8},{10,9},{11,1... | collective-permute-start | bytes 393224 | tf_op jit(solution)/shard_map/ppermute | solution.py:15
  42.8 14.4 %collective-permute-start.5 = (bf16[16,4096]{1,0:T(8,128)(2,1)S(1)}, bf16[16,4096]{1,0:T(8,128)(2,1)S(1)}, u32[]{:S(2)}, u32[]{:S(2)}) collective-permute-start(bf16[16,4096]{1,0:T(8,128)(2,1)S(1)} %copy-done.4), channel_id=1, source_target_pairs={{2,0},{3,1},{4,2},{5,3},{6,4},{7,5},{8,6},{9,7},{10,8},{11,9},{12,... | collective-permute-start | bytes 393224 | tf_op jit(solution)/shard_map/ppermute | solution.py:15
  49.3 9.9 %collective-permute-start.6 = (bf16[16,4096]{1,0:T(8,128)(2,1)S(1)}, bf16[16,4096]{1,0:T(8,128)(2,1)S(1)}, u32[]{:S(2)}, u32[]{:S(2)}) collective-permute-start(bf16[16,4096]{1,0:T(8,128)(2,1)S(1)} %copy-done.4), channel_id=1, source_target_pairs={{3,0},{4,1},{5,2},{6,3},{7,4},{8,5},{9,6},{10,7},{11,8},{12,9},{13... | collective-permute-start | bytes 393224 | tf_op jit(solution)/shard_map/ppermute | solution.py:15
  51.6 7.7 %collective-permute-start.7 = (bf16[16,4096]{1,0:T(8,128)(2,1)S(1)}, bf16[16,4096]{1,0:T(8,128)(2,1)S(1)}, u32[]{:S(2)}, u32[]{:S(2)}) collective-permute-start(bf16[16,4096]{1,0:T(8,128)(2,1)S(1)} %copy-done.4), channel_id=1, source_target_pairs={{4,0},{5,1},{6,2},{7,3},{8,4},{9,5},{10,6},{11,7},{12,8},{13,9},{1... | collective-permute-start | bytes 393224 | tf_op jit(solution)/shard_map/ppermute | solution.py:15
  55.3 120.4 %collective-permute-start.10 = (f32[16,16,256]{2,1,0:T(8,128)}, f32[16,16,256]{2,1,0:T(8,128)}, u32[]{:S(2)}, u32[]{:S(2)}) collective-permute-start(f32[16,16,256]{2,1,0:T(8,128)} %get-tuple-element.13), channel_id=1, source_target_pairs={{2,0},{3,1},{4,2},{5,3},{6,4},{7,5},{8,6},{9,7},{10,8},{11,9},{12,... | collective-permute-start | bytes 786440 | tf_op jit(solution)/shard_map/ppermute | solution.py:15
  57.1 119.8 %collective-permute-start.11 = (f32[16,16,256]{2,1,0:T(8,128)}, f32[16,16,256]{2,1,0:T(8,128)}, u32[]{:S(2)}, u32[]{:S(2)}) collective-permute-start(f32[16,16,256]{2,1,0:T(8,128)} %get-tuple-element.12), channel_id=1, source_target_pairs={{1,0},{2,1},{3,2},{4,3},{5,4},{6,5},{7,6},{8,7},{9,8},{10,9},{11,1... | collective-permute-start | bytes 786440 | tf_op jit(solution)/shard_map/ppermute | solution.py:15
  57.2 125.7 %collective-permute-start.12 = (f32[16,16,256]{2,1,0:T(8,128)}, f32[16,16,256]{2,1,0:T(8,128)}, u32[]{:S(2)}, u32[]{:S(2)}) collective-permute-start(f32[16,16,256]{2,1,0:T(8,128)} %get-tuple-element.11), channel_id=1, source_target_pairs={{127,0},{0,1},{1,2},{2,3},{3,4},{4,5},{5,6},{6,7},{7,8},{8,9},{9,1... | collective-permute-start | bytes 786440 | tf_op jit(solution)/shard_map/ppermute | solution.py:15
  59.3 134.4 %collective-permute-start.13 = (f32[16,16,256]{2,1,0:T(8,128)}, f32[16,16,256]{2,1,0:T(8,128)}, u32[]{:S(2)}, u32[]{:S(2)}) collective-permute-start(f32[16,16,256]{2,1,0:T(8,128)} %get-tuple-element.10), channel_id=1, source_target_pairs={{126,0},{127,1},{0,2},{1,3},{2,4},{3,5},{4,6},{5,7},{6,8},{7,9},{8... | collective-permute-start | bytes 786440 | tf_op jit(solution)/shard_map/ppermute | solution.py:15
  59.4 134.3 %collective-permute-start.14 = (f32[16,16,256]{2,1,0:T(8,128)}, f32[16,16,256]{2,1,0:T(8,128)}, u32[]{:S(2)}, u32[]{:S(2)}) collective-permute-start(f32[16,16,256]{2,1,0:T(8,128)} %get-tuple-element.9), channel_id=1, source_target_pairs={{125,0},{126,1},{127,2},{0,3},{1,4},{2,5},{3,6},{4,7},{5,8},{6,9},... | collective-permute-start | bytes 786440 | tf_op jit(solution)/shard_map/ppermute | solution.py:15
  169.7 13.3 %copy-start.5 = (f32[16,16,256]{2,1,0:T(8,128)S(1)}, f32[16,16,256]{2,1,0:T(8,128)}, u32[]{:S(2)}) copy-start(f32[16,16,256]{2,1,0:T(8,128)} %get-tuple-element.14) | copy-start | bytes 786436
  175.8 17.9 %collective-permute-start.15 = (f32[16,16,256]{2,1,0:T(8,128)S(1)}, f32[16,16,256]{2,1,0:T(8,128)S(1)}, u32[]{:S(2)}, u32[]{:S(2)}) collective-permute-start(f32[16,16,256]{2,1,0:T(8,128)S(1)} %copy-done.7), channel_id=1, source_target_pairs={{124,0},{125,1},{126,2},{127,3},{0,4},{1,5},{2,6},{3,7},{4,8},{5,9... | collective-permute-start | bytes 786440 | tf_op jit(solution)/shard_map/ppermute | solution.py:15
  177.0 16.7 %collective-permute-start.8 = (f32[16,16,256]{2,1,0:T(8,128)S(1)}, f32[16,16,256]{2,1,0:T(8,128)S(1)}, u32[]{:S(2)}, u32[]{:S(2)}) collective-permute-start(f32[16,16,256]{2,1,0:T(8,128)S(1)} %copy-done.6), channel_id=1, source_target_pairs={{4,0},{5,1},{6,2},{7,3},{8,4},{9,5},{10,6},{11,7},{12,8},{13,9},{1... | collective-permute-start | bytes 786440 | tf_op jit(solution)/shard_map/ppermute | solution.py:15
  183.0 10.8 %collective-permute-start.9 = (f32[16,16,256]{2,1,0:T(8,128)S(1)}, f32[16,16,256]{2,1,0:T(8,128)S(1)}, u32[]{:S(2)}, u32[]{:S(2)}) collective-permute-start(f32[16,16,256]{2,1,0:T(8,128)S(1)} %copy-done.5), channel_id=1, source_target_pairs={{3,0},{4,1},{5,2},{6,3},{7,4},{8,5},{9,6},{10,7},{11,8},{12,9},{13... | collective-permute-start | bytes 786440 | tf_op jit(solution)/shard_map/ppermute | solution.py:15
  (10 other events, 72.9 us)
Sparse Core Ops, SparseCore 0:
  10.2 78.0 all-gather.5
  91.5 64.1 all-gather.3
where the time goes:
time: 206 us; the launch traced here: 203 us
  waiting for transfers between devices  66.2 us (32%)
  local copies, waits for them, and re-layouts  43.2 us (21%)
  matrix products  37.6 us (18%)
  starting transfers between devices  32.3 us (16%)
  between operations  13.8 us (7%)
  other arithmetic  10.2 us (5%)
    all_gather x1, waiting for transfers between devices, shards(): piece = lax.all_gather(moments, 'surf', axis=0, tiled=True)  53.8 us
    ppermute x16, starting transfers between devices, from_behind(): return lax.ppermute(block, axis, route)  32.2 us
    all_gather x1, waiting for transfers between devices, shards(): lax.all_gather(upper_moments.reshape(parent_count, rank_count * rhs_count...  12.2 us
    dot_general x1, matrix products, shards(): jnp.einsum('qeb,eab->qea', remote, blocks, preferred_element_type=jnp.flo...  11 us
    dot_general x1, matrix products, shards(): jnp.einsum('ckrs,cksq->crq', coupling, picked.reshape(cluster_count, far_...  10.4 us
    gather x3, local copies, waits for them, and re-layouts, shards(): jnp.take(piece, jnp.clip(wanted, 0, piece.shape[0] - 1), axis=0)  9.31 us
    dot_general x1, matrix products, shards(): jnp.einsum('qea,eab->qeb', own_rows, blocks, preferred_element_type=jnp.f...  8.09 us
    reshape x1, local copies, waits for them, and re-layouts, shards(): leaf_coupling.reshape(cluster_count, far_count, rank_count, rank_count)  6.55 us
  transfers between devices with their start and end apart: 18, of which 3 were waited for; matrix products, arithmetic and copies ran while one was open for 42% of the time, Pallas kernels for 0%

commit v1 on v0

v1 whole, which is shorter than its diff:
```python
import jax
import jax.numpy as jnp
from jax import lax
from jax.experimental import pallas as pl
from jax.experimental.pallas import tpu as pltpu
from jax.sharding import PartitionSpec as P

HOPS = 4
OFFS = 2 * HOPS + 1
CHUNKS = 2
MESH = pl.DeviceIdType.MESH
F32 = jnp.float32
BF16 = jnp.bfloat16
NT = (((1,), (1,)), ((), ()))


def split(value):
    high = value.astype(BF16)
    return high, (value - high.astype(F32)).astype(BF16)


def dot_two(value, matrix, dims=(((1,), (0,)), ((), ()))):
    high, low = split(value)
    return lax.dot_general(high, matrix, dims, preferred_element_type=F32) + lax.dot_general(
        low, matrix, dims, preferred_element_type=F32
    )


def kernel(
    owner_ref,
    slot_ref,
    live_ref,
    far_leaf_ref,
    far_top_ref,
    signal_ref,
    basis_ref,
    transfer_ref,
    near_hbm,
    leaf_hbm,
    top_hbm,
    out_ref,
    near_buf,
    leaf_buf,
    top_buf,
    window,
    outgoing,
    hot_rows,
    hot,
    even_terms,
    odd_terms,
    partner_terms,
    far_terms,
    back_terms,
    table,
    sum_blocks,
    sum_children,
    leaf_acc,
    down_acc,
    near_sem,
    coup_sem,
    sig_send,
    sig_recv,
    ret_send,
    ret_recv,
    tab_send,
    tab_recv,
    par_send,
    par_recv,
):
    rhs = 16
    leaf = 256
    clusters = 16
    near = 8
    n = 128
    me = lax.axis_index("surf")
    core = lax.rem(me, 2)
    y = lax.rem(me // 2, 4)
    z = lax.rem(me // 8, 4)
    x = me // 32

    def at(px, pz, py):
        return ((px * 4 + pz) * 4 + py) * 2 + core

    def turn(value, step):
        return lax.rem(value + step + 4, 4)

    partner = me + 1 - 2 * core
    ahead = lax.rem(me + 2, n)
    behind = lax.rem(me + n - 2, n)
    y_up, y_down = at(x, z, turn(y, 1)), at(x, z, turn(y, -1))
    z_up, z_down = at(x, turn(z, 1), y), at(x, turn(z, -1), y)
    x_up, x_down = at(turn(x, 1), z, y), at(turn(x, -1), z, y)

    near_in = []
    for c in range(clusters):
        near_in.append(pltpu.make_async_copy(near_hbm.at[c], near_buf.at[c], near_sem.at[c]))
    leaf_in = pltpu.make_async_copy(leaf_hbm, leaf_buf, coup_sem.at[0])
    top_in = pltpu.make_async_copy(top_hbm, top_buf, coup_sem.at[1])
    for copy in near_in:
        copy.start()
    leaf_in.start()
    top_in.start()

    barrier = pltpu.get_barrier_semaphore()
    for peer in (partner, ahead, behind, y_up, y_down, z_up, z_down, x_up, x_down):
        pl.semaphore_signal(barrier, inc=1, device_id=(peer,), device_id_type=MESH)

    for c in range(clusters):
        window[HOPS * clusters + c] = signal_ref[:, c * leaf : (c + 1) * leaf]

    group = lax.broadcasted_iota(jnp.int32, (rhs, 128), 1) // 32
    row_id = lax.broadcasted_iota(jnp.int32, (1024, 128), 0)
    lane_id = lax.broadcasted_iota(jnp.int32, (1024, 128), 1)
    sum_blocks[...] = (row_id // 32 == lane_id % 32).astype(F32).astype(BF16)
    sum_children[...] = (row_id % 32 == lane_id).astype(F32).astype(BF16)

    @pl.loop(0, 4, init_carry=jnp.zeros((rhs, 128), F32))
    def upper_rows(p, upper):
        packed = jnp.zeros((rhs, 128), F32)
        lifted = [jnp.zeros((rhs, 128), F32) for _ in range(8)]
        for b in range(4):
            c = p * 4 + b
            columns = pl.ds(pl.multiple_of(c * leaf, leaf), leaf)
            shape = basis_ref[:, columns]
            moment = lax.dot_general(
                signal_ref[:, columns],
                jnp.concatenate([shape] * 4, axis=0),
                NT,
                preferred_element_type=F32,
            )
            packed = jnp.where(group == b, moment, packed)
            lift = transfer_ref[pl.ds(c, 1), :]
            lifted = [a + moment * lift[:, g * 128 : (g + 1) * 128] for g, a in enumerate(lifted)]
        table[x, z, y, core, p] = packed
        total = dot_two(jnp.concatenate(lifted, axis=1), sum_blocks[...])
        return jnp.where(group == p, total, upper)

    table[x, z, y, core, 4] = upper_rows

    pl.semaphore_wait(barrier, 9)

    def remote(src, dst, send, recv, device):
        return pltpu.make_async_remote_copy(
            src_ref=src,
            dst_ref=dst,
            send_sem=send,
            recv_sem=recv,
            device_id=(device,),
            device_id_type=MESH,
        )

    sent = []

    def start(copy):
        copy.start()
        sent.append(copy)
        return copy

    def place(offset):
        return window.at[pl.ds(offset * clusters, clusters)]

    def sig(src, dst, index, device):
        return start(remote(place(src), place(dst), sig_send.at[index], sig_recv.at[index], device))

    from_behind = sig(4, 2, 0, ahead)
    from_ahead = sig(4, 6, 1, behind)

    def tab(src, index, device):
        return start(remote(src, src, tab_send.at[index], tab_recv.at[index], device))

    own = table.at[x, z, y, core]
    y_from = [tab(own, 0, y_up), tab(own, 1, y_down)]

    def forward_y():
        for copy in y_from:
            copy.wait_recv()
        return [
            tab(table.at[x, z, turn(y, -1), core, pl.ds(0, 3)], 2, y_up),
            tab(table.at[x, z, turn(y, 1), core, pl.ds(3, 2)], 3, y_down),
        ]

    def par(src, index):
        return start(remote(src, src, par_send.at[index], par_recv.at[index], partner))

    lower, higher = pl.ds(0, 2), pl.ds(2, 2)

    def first_legs(copies):
        for copy in copies:
            copy.wait_recv()
        a = table.at[x, z, lower, core]
        b = table.at[x, z, higher, core]
        return [tab(a, 4, x_up), tab(a, 5, x_down), tab(b, 6, z_up), tab(b, 7, z_down)]

    def first_forwards(copies):
        for copy in copies:
            copy.wait_recv()
        return [
            tab(table.at[turn(x, -1), z, 0, core], 8, x_up),
            tab(table.at[turn(x, 1), z, 1, core], 9, x_down),
            tab(table.at[x, turn(z, -1), 2, core], 10, z_up),
            tab(table.at[x, turn(z, 1), 3, core], 11, z_down),
        ]

    def second_legs(copies):
        for copy in copies:
            copy.wait_recv()
        a = table.at[:, z, lower, core]
        b = table.at[x, :, higher, core]
        return [tab(a, 12, z_up), tab(a, 13, z_down), tab(b, 14, x_up), tab(b, 15, x_down)] + [
            par(a, 0),
            par(b, 1),
        ]

    def second_forwards(copies):
        for copy in copies[:4]:
            copy.wait_recv()
        more = [
            tab(table.at[:, turn(z, -1), 0, core], 16, z_up),
            tab(table.at[:, turn(z, 1), 1, core], 17, z_down),
            tab(table.at[turn(x, -1), :, 2, core], 18, x_up),
            tab(table.at[turn(x, 1), :, 3, core], 19, x_down),
        ]
        more += [
            par(table.at[:, turn(z, -1), lower, core], 2),
            par(table.at[:, turn(z, 1), lower, core], 3),
            par(table.at[turn(x, -1), :, higher, core], 4),
            par(table.at[turn(x, 1), :, higher, core], 5),
        ]
        return copies[4:] + more

    def last_pairs(copies):
        for copy in copies[2:6]:
            copy.wait_recv()
        return copies[:2] + copies[6:] + [
            par(table.at[:, turn(z, 2), lower, core], 6),
            par(table.at[turn(x, 2), :, higher, core], 7),
        ]

    window_row = lax.broadcasted_iota(jnp.int32, (1, 256), 1)

    def place_of(c, k):
        offset = lax.rem(owner_ref[c, k] - me + (HOPS + n), n)
        return jnp.minimum(offset, OFFS - 1) * clusters + slot_ref[c, k]

    def outward(first, count):
        for copy in near_in[first : first + count]:
            copy.wait()

        @pl.loop(first, first + count)
        def _(c):
            here = signal_ref[:, pl.ds(pl.multiple_of(c * leaf, leaf), leaf)]
            for k in range(near):
                rows = pl.ds(pl.multiple_of((c * near + k) * rhs, rhs), rhs)
                term = jnp.dot(here, near_buf[c, k], preferred_element_type=F32)
                outgoing[0, rows, :] = term[:, :128]
                outgoing[1, rows, :] = term[:, 128:]
                target = place_of(c, k) + (1 - live_ref[c, k]) * 256
                hot_rows[pl.ds(c * near + k, 1), :] = jnp.where(window_row == target, 1.0, 0.0)

    def scatter(first, count):
        @pl.loop(first, first + count)
        def _(q):
            picks = pl.ds(q, clusters * near, stride=rhs)
            terms = jnp.concatenate([outgoing[0, picks, :], outgoing[1, picks, :]], axis=1)
            high, low = split(terms)
            summed = jnp.dot(
                hot[...], jnp.concatenate([high, low], axis=0), preferred_element_type=F32
            )
            rows = pl.ds(pl.multiple_of(q * clusters, clusters), clusters)
            for offset in range(OFFS):
                terms_ref = odd_terms if offset % 2 else even_terms
                block = summed[offset * clusters : (offset + 1) * clusters, :]
                terms_ref[offset // 2, 0, rows, :] = block[:, :128]
                terms_ref[offset // 2, 1, rows, :] = block[:, 128:]

    height = rhs * clusters // CHUNKS

    def part(h):
        return pl.ds(h * height, height)

    def ret(src, dst, index, device):
        return start(remote(src, dst, ret_send.at[index], ret_recv.at[index], device))

    def to_partner(h):
        return ret(odd_terms.at[:, :, part(h)], partner_terms.at[:, :, part(h)], 5 * h, partner)

    def to_far(h, copy):
        copy.wait_recv()
        rows = part(h)
        for i in range(4):
            slot = i + 1 - core
            even_terms[slot, :, rows, :] = even_terms[slot, :, rows, :] + partner_terms[i, :, rows, :]
        return [
            ret(even_terms.at[4, :, rows], far_terms.at[0, :, rows], 5 * h + 1, ahead),
            ret(even_terms.at[0, :, rows], far_terms.at[1, :, rows], 5 * h + 2, behind),
        ]

    def to_next(h, copies):
        rows = part(h)
        copies[0].wait_recv()
        even_terms[3, :, rows, :] = even_terms[3, :, rows, :] + far_terms[0, :, rows, :]
        up = ret(even_terms.at[3, :, rows], back_terms.at[0, :, rows], 5 * h + 3, ahead)
        copies[1].wait_recv()
        even_terms[1, :, rows, :] = even_terms[1, :, rows, :] + far_terms[1, :, rows, :]
        down = ret(even_terms.at[1, :, rows], back_terms.at[1, :, rows], 5 * h + 4, behind)
        return [up, down]

    def inward(first, count):
        @pl.loop(first, first + count)
        def _(c):
            total = jnp.zeros((rhs, leaf), F32)
            for k in range(near):
                there = window[place_of(c, k)]
                there = (there.astype(F32) * live_ref[c, k].astype(F32)).astype(BF16)
                total = total + lax.dot_general(
                    there, near_buf[c, k], NT, preferred_element_type=F32
                )
            out_ref[:, pl.ds(pl.multiple_of(c * leaf, leaf), leaf)] = total

    def picked(device, block, quarter):
        tile = table[device >> 5, (device >> 3) & 3, (device >> 1) & 3, device & 1, block]
        tile = jnp.where(group == quarter, tile, 0.0)
        tile = tile + pltpu.roll(tile, 32, 1)
        return tile + pltpu.roll(tile, 64, 1)

    def coupled(buf, row, pick):
        def step(k, sums):
            tile = pick(k)
            factors = buf[row, pl.ds(k, 1), :]
            return tuple(
                a + tile * factors[:, g * 128 : (g + 1) * 128] for g, a in enumerate(sums)
            )

        sums = lax.fori_loop(
            0, 32, step, tuple(jnp.zeros((rhs, 128), F32) for _ in range(8)), unroll=4
        )
        return jnp.concatenate(sums, axis=1)

    def far(first, count):
        @pl.loop(first, first + count)
        def _(p):
            def pick_top(k):
                j = far_top_ref[p, k]
                return picked(j >> 2, 4, j & 3)

            top = dot_two(coupled(top_buf, p, pick_top), sum_blocks[...])[:, :32]
            spread = dot_two(top, sum_blocks[:, :32], NT)

            @pl.loop(0, 4)
            def _(b):
                c = p * 4 + b

                def pick_leaf(k):
                    j = far_leaf_ref[c, k]
                    return picked(j >> 4, (j >> 2) & 3, j & 3)

                rows = pl.ds(pl.multiple_of(b * rhs, rhs), rhs)
                leaf_acc[rows, :] = coupled(leaf_buf, c, pick_leaf)
                down_acc[rows, :] = spread * transfer_ref[pl.ds(c, 1), :]

            field = dot_two(leaf_acc[...], sum_blocks[...]) + dot_two(
                down_acc[...], sum_children[...]
            )
            field = field[:, :32].astype(BF16)
            for b in range(4):
                columns = pl.ds(pl.multiple_of((p * 4 + b) * leaf, leaf), leaf)
                out_ref[:, columns] = out_ref[:, columns] + jnp.dot(
                    field[b * rhs : (b + 1) * rhs], basis_ref[:, columns], preferred_element_type=F32
                )

    own_to_partner = sig(4, 3 + 2 * core, 2, partner)
    outward(0, 2)
    y_more = forward_y()
    outward(2, 4)
    from_behind.wait_recv()
    from_ahead.wait_recv()
    second_behind = sig(2, 0, 3, ahead)
    second_ahead = sig(6, 8, 4, behind)
    near_pairs = [
        sig(2, 1 + 2 * core, 5, partner),
        sig(6, 5 + 2 * core, 6, partner),
    ]
    legs = first_legs(y_more)
    outward(6, 4)
    legs = first_forwards(legs)
    outward(10, 6)
    legs = second_legs(legs)
    second_behind.wait_recv()
    second_ahead.wait_recv()
    last_pair = sig(8 - 8 * core, 7 - 6 * core, 7, partner)
    flipped = hot_rows[...].T.astype(BF16)
    hot[...] = jnp.concatenate([flipped, flipped], axis=1)[: OFFS * clusters, :]
    stage = []
    for h in range(CHUNKS):
        scatter(h * rhs // CHUNKS, rhs // CHUNKS)
        stage.append(to_partner(h))
    for copy in [own_to_partner, last_pair] + near_pairs:
        copy.wait_recv()
    legs = second_forwards(legs)
    inward(0, 4)
    stage = [to_far(h, copy) for h, copy in enumerate(stage)]
    inward(4, 4)
    legs = last_pairs(legs)
    inward(8, 8)
    stage = [to_next(h, copies) for h, copies in enumerate(stage)]
    leaf_in.wait()
    top_in.wait()
    for copy in legs:
        copy.wait_recv()
    far(0, 4)
    for copies in stage:
        for copy in copies:
            copy.wait_recv()

    @pl.loop(0, clusters)
    def _(c):
        rows = pl.ds(c, rhs, stride=clusters)
        for half in range(2):
            columns = pl.ds(pl.multiple_of(c * leaf + half * 128, 128), 128)
            total = out_ref[:, columns] + even_terms[2, half, rows, :]
            out_ref[:, columns] = (
                total + back_terms[0, half, rows, :] + back_terms[1, half, rows, :]
            )

    for copy in sent:
        copy.wait_send()


def shards(
    signal,
    near_blocks,
    near_owner,
    near_slot,
    near_live,
    leaf_basis,
    transfer,
    leaf_coupling,
    far_leaf,
    top_coupling,
    far_top,
):
    smem = pl.BlockSpec(memory_space=pltpu.SMEM)
    vmem = pl.BlockSpec(memory_space=pltpu.VMEM)
    hbm = pl.BlockSpec(memory_space=pl.ANY)
    dma = pltpu.SemaphoreType.DMA
    return pl.pallas_call(
        kernel,
        out_shape=jax.ShapeDtypeStruct((16, 4096), F32),
        in_specs=[smem] * 5 + [vmem] * 3 + [hbm] * 3,
        out_specs=vmem,
        scratch_shapes=[
            pltpu.VMEM((16, 8, 256, 256), BF16),
            pltpu.VMEM((16, 32, 1024), F32),
            pltpu.VMEM((4, 32, 1024), F32),
            pltpu.VMEM((OFFS * 16, 16, 256), BF16),
            pltpu.VMEM((2, 2048, 128), F32),
            pltpu.VMEM((128, 256), F32),
            pltpu.VMEM((OFFS * 16, 256), BF16),
            pltpu.VMEM((5, 2, 256, 128), F32),
            pltpu.VMEM((4, 2, 256, 128), F32),
            pltpu.VMEM((4, 2, 256, 128), F32),
            pltpu.VMEM((2, 2, 256, 128), F32),
            pltpu.VMEM((2, 2, 256, 128), F32),
            pltpu.VMEM((4, 4, 4, 2, 5, 16, 128), F32),
            pltpu.VMEM((1024, 128), BF16),
            pltpu.VMEM((1024, 128), BF16),
            pltpu.VMEM((64, 1024), F32),
            pltpu.VMEM((64, 1024), F32),
            dma((16,)),
            dma((2,)),
            dma((8,)),
            dma((8,)),
            dma((5 * CHUNKS,)),
            dma((5 * CHUNKS,)),
            dma((20,)),
            dma((20,)),
            dma((8,)),
            dma((8,)),
        ],
        compiler_params=pltpu.CompilerParams(
            collective_id=0, has_side_effects=True, vmem_limit_bytes=52 * 1024 * 1024
        ),
        cost_estimate=pl.CostEstimate(
            flops=1200000000, bytes_accessed=20000000, transcendentals=0
        ),
    )(
        near_owner,
        near_slot,
        near_live,
        far_leaf,
        far_top,
        signal,
        leaf_basis,
        transfer,
        near_blocks,
        leaf_coupling,
        top_coupling,
    )


def solution(mesh):
    placed = (
        P(None, "surf"),
        P("surf", None, None, None),
        P("surf", None),
        P("surf", None),
        P("surf", None),
        P(None, "surf"),
        P("surf", None),
        P("surf", None, None),
        P("surf", None),
        P("surf", None, None),
        P("surf", None),
    )
    return jax.shard_map(
        shards, mesh=mesh, in_specs=placed, out_specs=P(None, "surf"), check_vma=False
    )
```

time: 206 us -> 92.1 us (0.45)
  the two profiles are of different devices: /device:TPU:1 before, /device:TPU:38 now
where the time goes in v1:
time: 92.1 us; the launch traced here: 91.7 us
  Pallas kernels  83.6 us (91%)
  local copies, waits for them, and re-layouts  8.09 us (9%)
    pallas_call x1, Pallas kernels, shards(): pl.pallas_call(kernel, out_shape=jax.ShapeDtypeStruct((16, 4096), F32), i...  83.6 us
    unnamed x16, local copies, waits for them, and re-layouts  8.09 us

profile of v1, /device:TPU:38, one launch (start us, length us, event | category | flops | bytes accessed | tf_op | source)
XLA Modules:
  0.0 91.7 jit_solution(10230477122942280978)
XLA Ops:
  0.0 0.8 copy.12.owner_ref
  0.8 0.8 copy.13.slot_ref
  1.5 0.8 copy.14.live_ref
  2.3 0.0 copy-start
  2.3 1.0 %copy-done = f32[4,32,1024]{2,1,0:T(8,128)S(1)} copy-done((f32[4,32,1024]{2,1,0:T(8,128)S(1)}, f32[4,32,1024]{2,1,0:T(8,128)}, u32[]{:S(2)}) %copy-start) | copy-done | bytes 524312
  3.3 0.0 copy-start.1
  3.3 0.9 %copy-done.1 = bf16[32,4096]{1,0:T(8,128)(2,1)S(1)} copy-done((bf16[32,4096]{1,0:T(8,128)(2,1)S(1)}, bf16[32,4096]{1,0:T(8,128)(2,1)}, u32[]{:S(2)}) %copy-start.1) | copy-done | bytes 262168
  4.3 0.0 copy-start.2
  4.3 0.9 copy-done.2
  5.2 0.0 copy-start.3
  5.2 0.8 copy-done.3
  6.0 0.0 copy-start.4
  6.0 0.7 copy-done.4
  6.7 0.0 copy-start.5
  6.7 0.7 copy-done.5
  7.4 83.6 %shard_map.109 = f32[16,4096]{1,0:T(8,128)S(1)} custom-call(s32[16,8]{1,0:T(8,128)S(1)} %copy.12.owner_ref, s32[16,8]{1,0:T(8,128)S(1)} %copy.13.slot_ref, s32[16,8]{1,0:T(8,128)S(1)} %copy.14.live_ref, s32[16,32]{1,0:T(8,128)S(1)} %copy-done.4, s32[4,32]{1,0:T(4,128)S(1)} %copy-done.5, bf16[16,4096]{1,0:T(8,128)(2,1)S(1)} %copy-done.2, ...), custom_call_target="tpu_custom_call" | custom-call | flops 1200000000 | bytes 20000000 | tf_op jit(solution)/shard_map/pallas_call | solution.py:446
  91.0 0.7 copy.16
Async XLA Ops:
  2.3 1.0 %copy-start = (f32[4,32,1024]{2,1,0:T(8,128)S(1)}, f32[4,32,1024]{2,1,0:T(8,128)}, u32[]{:S(2)}) copy-start(f32[4,32,1024]{2,1,0:T(8,128)} %top_hbm.1) | copy-start | bytes 1572868
  3.3 0.9 %copy-start.1 = (bf16[32,4096]{1,0:T(8,128)(2,1)S(1)}, bf16[32,4096]{1,0:T(8,128)(2,1)}, u32[]{:S(2)}) copy-start(bf16[32,4096]{1,0:T(8,128)(2,1)} %basis_ref.1) | copy-start | bytes 786436
  4.3 0.9 copy-start.2
  5.2 0.8 copy-start.3
  6.0 0.7 copy-start.4
  6.7 0.7 copy-start.5

commit v2 on v1

v2 whole, which is shorter than its diff:
```python
import jax
import jax.numpy as jnp
from jax import lax
from jax.experimental import pallas as pl
from jax.experimental.pallas import tpu as pltpu
from jax.sharding import PartitionSpec as P

HOPS = 4
OFFS = 2 * HOPS + 1
LEAST = -24.0
STEPS = 800.0
MESH = pl.DeviceIdType.MESH
F32 = jnp.float32
BF16 = jnp.bfloat16
NT = (((1,), (1,)), ((), ()))


def split(value):
    high = value.astype(BF16)
    return high, (value - high.astype(F32)).astype(BF16)


def dot_two(value, matrix, dims=(((1,), (0,)), ((), ()))):
    high, low = split(value)
    return lax.dot_general(high, matrix, dims, preferred_element_type=F32) + lax.dot_general(
        low, matrix, dims, preferred_element_type=F32
    )


def encode(value):
    level = (jnp.log2(jnp.maximum(jnp.abs(value), 2.0**LEAST)) - LEAST) * STEPS
    level = jnp.round(jnp.minimum(level, 32767.0))
    return jnp.where(value < 0, -level, level).astype(jnp.int32).astype(jnp.int16)


def decode(level):
    size = jnp.exp2(jnp.abs(level) * (1.0 / STEPS) + LEAST)
    return jnp.where(level < 0, -size, jnp.where(level > 0, size, 0.0))


def kernel(
    owner_hbm,
    slot_hbm,
    live_hbm,
    far_leaf_hbm,
    far_top_hbm,
    signal_hbm,
    basis_hbm,
    transfer_hbm,
    near_hbm,
    leaf_hbm,
    top_hbm,
    out_ref,
    owner_ref,
    slot_ref,
    live_ref,
    far_leaf_ref,
    far_top_ref,
    signal_ref,
    basis_ref,
    transfer_ref,
    near_buf,
    leaf_buf,
    top_buf,
    window,
    outgoing,
    hot_rows,
    hot,
    even_terms,
    odd_terms,
    partner_terms,
    codes_out,
    codes_in,
    table,
    tiles,
    sum_blocks,
    sum_children,
    leaf_acc,
    down_acc,
    near_sem,
    load_sem,
    sig_send,
    sig_recv,
    ret_send,
    ret_recv,
    tab_send,
    tab_recv,
    par_send,
    par_recv,
):
    rhs = 16
    leaf = 256
    clusters = 16
    near = 8
    n = 128
    me = lax.axis_index("surf")
    core = lax.rem(me, 2)
    y = lax.rem(me // 2, 4)
    z = lax.rem(me // 8, 4)
    x = me // 32

    def at(px, pz, py):
        return ((px * 4 + pz) * 4 + py) * 2 + core

    def turn(value, step):
        return lax.rem(value + step + 4, 4)

    def along(step):
        return lax.rem(me + step + n, n)

    partner = me + 1 - 2 * core
    steps = (1, -1, 2)
    y_peers = [at(x, z, turn(y, step)) for step in steps]
    z_peers = [at(x, turn(z, step), y) for step in steps]
    x_peers = [at(turn(x, step), z, y) for step in steps]
    surf_peers = [along(step) for step in (-4, -2, 2, 4)]

    loads = [
        pltpu.make_async_copy(src, dst, load_sem.at[i])
        for i, (src, dst) in enumerate(
            (
                (signal_hbm, signal_ref),
                (basis_hbm, basis_ref),
                (transfer_hbm, transfer_ref),
                (owner_hbm, owner_ref),
                (slot_hbm, slot_ref),
                (live_hbm, live_ref),
                (far_leaf_hbm, far_leaf_ref),
                (far_top_hbm, far_top_ref),
                (leaf_hbm, leaf_buf),
                (top_hbm, top_buf),
            )
        )
    ]
    near_in = [
        pltpu.make_async_copy(near_hbm.at[c], near_buf.at[c], near_sem.at[c])
        for c in range(clusters)
    ]
    for copy in loads[:3]:
        copy.start()
    barrier = pltpu.get_barrier_semaphore()
    peers = [partner] + surf_peers + y_peers + z_peers + x_peers
    for peer in peers:
        pl.semaphore_signal(barrier, inc=1, device_id=(peer,), device_id_type=MESH)
    for copy in loads[3:8] + near_in + loads[8:]:
        copy.start()

    group = lax.broadcasted_iota(jnp.int32, (rhs, 128), 1) // 32
    row_id = lax.broadcasted_iota(jnp.int32, (1024, 128), 0)
    lane_id = lax.broadcasted_iota(jnp.int32, (1024, 128), 1)
    sum_blocks[...] = (row_id // 32 == lane_id % 32).astype(F32).astype(BF16)
    sum_children[...] = (row_id % 32 == lane_id % 32).astype(F32).astype(BF16)

    loads[0].wait()
    for c in range(clusters):
        window[HOPS * clusters + c] = signal_ref[:, c * leaf : (c + 1) * leaf]
    loads[1].wait()
    loads[2].wait()

    upper = jnp.zeros((rhs, 128), F32)
    for p in range(4):
        packed = jnp.zeros((rhs, 128), F32)
        lifted = [jnp.zeros((rhs, 128), F32) for _ in range(8)]
        for b in range(4):
            c = p * 4 + b
            columns = slice(c * leaf, (c + 1) * leaf)
            shape = basis_ref[:, columns]
            moment = lax.dot_general(
                signal_ref[:, columns],
                jnp.concatenate([shape] * 4, axis=0),
                NT,
                preferred_element_type=F32,
            )
            packed = jnp.where(group == b, moment, packed)
            lift = transfer_ref[c : c + 1, :]
            lifted = [a + moment * lift[:, g * 128 : (g + 1) * 128] for g, a in enumerate(lifted)]
        table[x, z, y, core, p] = encode(packed)
        total = dot_two(jnp.concatenate(lifted, axis=1), sum_blocks[...])
        upper = jnp.where(group == p, total, upper)
    table[x, z, y, core, 4] = encode(upper)

    pl.semaphore_wait(barrier, len(peers))

    def remote(src, dst, send, recv, device):
        return pltpu.make_async_remote_copy(
            src_ref=src,
            dst_ref=dst,
            send_sem=send,
            recv_sem=recv,
            device_id=(device,),
            device_id_type=MESH,
        )

    sent = []

    def start(copy):
        copy.start()
        sent.append(copy)
        return copy

    def arrived(copies):
        for copy in copies:
            copy.wait_recv()

    def tab(src, index, device):
        return start(remote(src, src, tab_send.at[index], tab_recv.at[index], device))

    def par(src, index):
        return start(remote(src, src, par_send.at[index], par_recv.at[index], partner))

    def place(offset):
        return window.at[pl.ds(offset * clusters, clusters)]

    def sig(src, dst, index, device):
        return start(remote(place(src), place(dst), sig_send.at[index], sig_recv.at[index], device))

    def rows_along_y():
        own = table.at[x, z, y, core]
        return [tab(own, i, peer) for i, peer in enumerate(y_peers)]

    def rows_out(copies):
        arrived(copies)
        row = table.at[x, z, :, core]
        return [tab(row, 3 + i, peer) for i, peer in enumerate(x_peers)] + [
            tab(row, 6 + i, peer) for i, peer in enumerate(z_peers)
        ]

    def halves_out(copies):
        more = []
        for i, step in enumerate(steps):
            copies[i].wait_recv()
            half = table.at[turn(x, -step), z, pl.ds(0, 2), core]
            more += [tab(half, 9 + 3 * i + j, peer) for j, peer in enumerate(z_peers)]
            copies[3 + i].wait_recv()
            half = table.at[x, turn(z, -step), pl.ds(2, 2), core]
            more += [tab(half, 18 + 3 * i + j, peer) for j, peer in enumerate(x_peers)]
        return more + [par(table.at[:, z, :, core], 0)]

    def to_other_core(copies):
        for j, step in enumerate(steps):
            arrived([copies[6 * i + j] for i in range(3)])
            arrived([copies[6 * j + 3 + i] for i in range(3)])
            copies.append(par(table.at[:, turn(z, -step), :, core], 1 + j))
        return copies[18:]

    window_row = lax.broadcasted_iota(jnp.int32, (1, 256), 1)

    def place_of(c, k):
        offset = lax.rem(owner_ref[k, c] - me + (HOPS + n), n)
        return jnp.minimum(offset, OFFS - 1) * clusters + slot_ref[k, c]

    def outward(first, count):
        for copy in near_in[first : first + count]:
            copy.wait()

        @pl.loop(first, first + count)
        def _(c):
            here = signal_ref[:, pl.ds(pl.multiple_of(c * leaf, leaf), leaf)]
            for k in range(near):
                rows = pl.ds(pl.multiple_of((c * near + k) * rhs, rhs), rhs)
                term = jnp.dot(here, near_buf[c, k], preferred_element_type=F32)
                outgoing[0, rows, :] = term[:, :128]
                outgoing[1, rows, :] = term[:, 128:]
                target = place_of(c, k) + (1 - live_ref[k, c]) * 256
                hot_rows[pl.ds(c * near + k, 1), :] = jnp.where(window_row == target, 1.0, 0.0)

    def scatter(half):
        @pl.loop(0, rhs // 2)
        def _(pair):
            terms = jnp.concatenate(
                [
                    outgoing[half, pl.ds(pair * 2 + i, clusters * near, stride=rhs), :]
                    for i in range(2)
                ],
                axis=1,
            )
            high, low = split(terms)
            summed = jnp.dot(
                hot[...], jnp.concatenate([high, low], axis=0), preferred_element_type=F32
            )
            for i in range(2):
                rows = pl.ds(pl.multiple_of((pair * 2 + i) * clusters, clusters), clusters)
                for offset in range(OFFS):
                    terms_ref = odd_terms if offset % 2 else even_terms
                    terms_ref[offset // 2, half, rows, :] = summed[
                        offset * clusters : (offset + 1) * clusters, i * 128 : (i + 1) * 128
                    ]

    def ret(src, dst, index, device):
        return start(remote(src, dst, ret_send.at[index], ret_recv.at[index], device))

    def to_partner(half):
        return ret(odd_terms.at[:, half], partner_terms.at[:, half], 5 * half, partner)

    height = rhs * clusters

    def to_targets(half, copy):
        copy.wait_recv()
        copies = []
        for i, offset in enumerate((0, 1, 3, 4)):
            j = offset - 1 + core
            valid = jnp.logical_and(j >= 0, j <= 3)
            weight = jnp.where(valid, 1.0, 0.0)
            summed = (
                even_terms[offset, half]
                + partner_terms[jnp.clip(j, 0, 3), half] * weight
            )
            peak = jnp.maximum(jnp.max(jnp.abs(summed), keepdims=True), 2.0**-100)
            power = jnp.ceil(jnp.log2(peak * (1.0 / 32000.0)))
            codes_out[i, half, :height] = (
                jnp.round(summed * jnp.exp2(-power)).astype(jnp.int32).astype(jnp.int16)
            )
            codes_out[i, half, height:] = (
                jnp.broadcast_to(power, (16, 128)).astype(jnp.int32).astype(jnp.int16)
            )
            copies.append(
                ret(codes_out.at[i, half], codes_in.at[i, half], 5 * half + 1 + i, surf_peers[i])
            )
        even_terms[2, half] = even_terms[2, half] + partner_terms[1 + core, half]
        return copies

    def add_returned(half, copies):
        total = even_terms[2, half]
        for i, copy in enumerate(copies):
            copy.wait_recv()
            power = codes_in[i, half, height:].astype(jnp.int32).astype(F32)[:1]
            total = total + codes_in[i, half, :height].astype(jnp.int32).astype(F32) * jnp.exp2(
                power
            )
        even_terms[2, half] = total

    def inward(first, count):
        @pl.loop(first, first + count)
        def _(c):
            total = jnp.zeros((rhs, leaf), F32)
            for k in range(near):
                there = window[place_of(c, k)]
                there = (there.astype(F32) * live_ref[k, c].astype(F32)).astype(BF16)
                total = total + lax.dot_general(
                    there, near_buf[c, k], NT, preferred_element_type=F32
                )
            out_ref[:, pl.ds(pl.multiple_of(c * leaf, leaf), leaf)] = total

    def picked(device, block, quarter):
        tile = table[device >> 5, (device >> 3) & 3, (device >> 1) & 3, device & 1, block]
        level = tile.astype(jnp.int32).astype(F32)
        return split(decode(jnp.where(group == quarter, level, 0.0)))

    def coupled(buf, row, pick):
        for first in (0, 16):
            pairs = [pick(first + k) for k in range(16)]
            both = jnp.concatenate(
                [jnp.concatenate([pair[i] for pair in pairs], axis=0) for i in range(2)], axis=1
            )
            tiles[first * rhs : (first + 16) * rhs, :] = jnp.dot(
                both, sum_children[:256, :], preferred_element_type=F32
            )

        def step(eight, sums):
            factors = buf[row, pl.ds(pl.multiple_of(eight * 8, 8), 8), :]
            for k in range(8):
                tile = tiles[pl.ds(pl.multiple_of((eight * 8 + k) * rhs, rhs), rhs), :]
                sums = tuple(
                    a + tile * factors[k : k + 1, g * 128 : (g + 1) * 128]
                    for g, a in enumerate(sums)
                )
            return sums

        sums = lax.fori_loop(0, 4, step, tuple(jnp.zeros((rhs, 128), F32) for _ in range(8)))
        return jnp.concatenate(sums, axis=1)

    def far(first, count):
        @pl.loop(first, first + count)
        def _(p):
            def pick_top(k):
                j = far_top_ref[p, k]
                return picked(j >> 2, 4, j & 3)

            top = dot_two(coupled(top_buf, p, pick_top), sum_blocks[...])[:, :32]
            spread = dot_two(top, sum_blocks[:, :32], NT)

            @pl.loop(0, 4)
            def _(b):
                c = p * 4 + b

                def pick_leaf(k):
                    j = far_leaf_ref[c, k]
                    return picked(j >> 4, (j >> 2) & 3, j & 3)

                rows = pl.ds(pl.multiple_of(b * rhs, rhs), rhs)
                leaf_acc[rows, :] = coupled(leaf_buf, c, pick_leaf)
                down_acc[rows, :] = spread * transfer_ref[pl.ds(c, 1), :]

            field = dot_two(leaf_acc[...], sum_blocks[...]) + dot_two(
                down_acc[...], sum_children[...]
            )
            field = field[:, :32].astype(BF16)
            for b in range(4):
                columns = pl.ds(pl.multiple_of((p * 4 + b) * leaf, leaf), leaf)
                out_ref[:, columns] = out_ref[:, columns] + jnp.dot(
                    field[b * rhs : (b + 1) * rhs], basis_ref[:, columns], preferred_element_type=F32
                )

    legs = rows_along_y()
    signals = [
        sig(4, 8, 0, surf_peers[0]),
        sig(4, 6, 1, surf_peers[1]),
        sig(4, 2, 2, surf_peers[2]),
        sig(4, 0, 3, surf_peers[3]),
    ]
    pairs = [sig(4, 3 + 2 * core, 4, partner)]
    for copy in loads[3:6]:
        copy.wait()
    outward(0, 5)
    legs = rows_out(legs)
    outward(5, 11)
    flipped = hot_rows[...].T.astype(BF16)
    hot[...] = jnp.concatenate([flipped, flipped], axis=1)[: OFFS * clusters, :]
    scatter(0)
    stage = [to_partner(0)]
    scatter(1)
    stage.append(to_partner(1))
    legs = halves_out(legs)
    arrived(signals)
    pairs += [
        sig(2, 1 + 2 * core, 5, partner),
        sig(6, 5 + 2 * core, 6, partner),
        sig(8 - 8 * core, 7 - 6 * core, 7, partner),
    ]
    stage = [to_targets(half, copy) for half, copy in enumerate(stage)]
    arrived(pairs)
    inward(0, 12)
    legs = to_other_core(legs)
    inward(12, 4)
    for copy in loads[6:]:
        copy.wait()
    arrived(legs)
    far(0, 4)
    for half, copies in enumerate(stage):
        add_returned(half, copies)

    @pl.loop(0, clusters)
    def _(c):
        rows = pl.ds(c, rhs, stride=clusters)
        for half in range(2):
            columns = pl.ds(pl.multiple_of(c * leaf + half * 128, 128), 128)
            out_ref[:, columns] = out_ref[:, columns] + even_terms[2, half, rows, :]

    for copy in sent:
        copy.wait_send()


def shards(
    signal,
    near_blocks,
    near_owner,
    near_slot,
    near_live,
    leaf_basis,
    transfer,
    leaf_coupling,
    far_leaf,
    top_coupling,
    far_top,
):
    hbm = pl.BlockSpec(memory_space=pl.ANY)
    dma = pltpu.SemaphoreType.DMA
    return pl.pallas_call(
        kernel,
        out_shape=jax.ShapeDtypeStruct((16, 4096), F32),
        in_specs=[hbm] * 11,
        out_specs=pl.BlockSpec(memory_space=pltpu.VMEM),
        scratch_shapes=[
            pltpu.SMEM((8, 16), jnp.int32),
            pltpu.SMEM((8, 16), jnp.int32),
            pltpu.SMEM((8, 16), jnp.int32),
            pltpu.SMEM((16, 32), jnp.int32),
            pltpu.SMEM((4, 32), jnp.int32),
            pltpu.VMEM((16, 4096), BF16),
            pltpu.VMEM((32, 4096), BF16),
            pltpu.VMEM((16, 1024), F32),
            pltpu.VMEM((16, 8, 256, 256), BF16),
            pltpu.VMEM((16, 32, 1024), F32),
            pltpu.VMEM((4, 32, 1024), F32),
            pltpu.VMEM((OFFS * 16, 16, 256), BF16),
            pltpu.VMEM((2, 2048, 128), F32),
            pltpu.VMEM((128, 256), F32),
            pltpu.VMEM((OFFS * 16, 256), BF16),
            pltpu.VMEM((5, 2, 256, 128), F32),
            pltpu.VMEM((4, 2, 256, 128), F32),
            pltpu.VMEM((4, 2, 256, 128), F32),
            pltpu.VMEM((4, 2, 272, 128), jnp.int16),
            pltpu.VMEM((4, 2, 272, 128), jnp.int16),
            pltpu.VMEM((4, 4, 4, 2, 5, 16, 128), jnp.int16),
            pltpu.VMEM((512, 128), F32),
            pltpu.VMEM((1024, 128), BF16),
            pltpu.VMEM((1024, 128), BF16),
            pltpu.VMEM((64, 1024), F32),
            pltpu.VMEM((64, 1024), F32),
            dma((16,)),
            dma((10,)),
            dma((8,)),
            dma((8,)),
            dma((10,)),
            dma((10,)),
            dma((27,)),
            dma((27,)),
            dma((4,)),
            dma((4,)),
        ],
        compiler_params=pltpu.CompilerParams(
            collective_id=0, has_side_effects=True, vmem_limit_bytes=62 * 1024 * 1024
        ),
        cost_estimate=pl.CostEstimate(
            flops=1200000000, bytes_accessed=20000000, transcendentals=0
        ),
    )(
        near_owner.T,
        near_slot.T,
        near_live.T,
        far_leaf,
        far_top,
        signal,
        leaf_basis,
        transfer,
        near_blocks,
        leaf_coupling,
        top_coupling,
    )


def solution(mesh):
    placed = (
        P(None, "surf"),
        P("surf", None, None, None),
        P("surf", None),
        P("surf", None),
        P("surf", None),
        P(None, "surf"),
        P("surf", None),
        P("surf", None, None),
        P("surf", None),
        P("surf", None, None),
        P("surf", None),
    )
    return jax.shard_map(
        shards, mesh=mesh, in_specs=placed, out_specs=P(None, "surf"), check_vma=False
    )
```

time: 92.1 us -> 55.3 us (0.60)
  the two profiles are of different devices: /device:TPU:38 before, /device:TPU:1 now
where the time goes in v2:
time: 55.3 us; the launch traced here: 55.2 us
  Pallas kernels  53.5 us (97%)
  local copies, waits for them, and re-layouts  1.67 us (3%)
    pallas_call x1, Pallas kernels, shards(): pl.pallas_call(kernel, out_shape=jax.ShapeDtypeStruct((16, 4096), F32), i...  53.5 us
    unnamed x1, local copies, waits for them, and re-layouts  1.67 us

profile of v2, /device:TPU:1, one launch (start us, length us, event | category | flops | bytes accessed | tf_op | source)
XLA Modules:
  0.0 55.2 jit_solution(16384653071734066771)
XLA Ops:
  0.0 53.5 %shard_map.109 = f32[16,4096]{1,0:T(8,128)} custom-call(s32[8,16]{1,0:T(8,128)} %bitcast.3, s32[8,16]{1,0:T(8,128)} %bitcast.4, s32[8,16]{1,0:T(8,128)} %bitcast.5, s32[16,32]{1,0:T(8,128)} %far_leaf_hbm.1, s32[4,32]{1,0:T(4,128)} %far_top_hbm.1, bf16[16,4096]{1,0:T(8,128)(2,1)} %signal_hbm.1, bf16[32,4096]{1,0:T(8,128)(2,1)} %basis_hbm.1, ...), custom_call_target="tpu_custom_call" | custom-call | flops 1200000000 | bytes 20000000 | tf_op jit(solution)/shard_map/pallas_call | solution.py:468
  53.5 1.7 %copy.13 = f32[16,4096]{1,0:T(8,128)} copy(f32[16,4096]{1,0:T(8,128)} %shard_map.109) | data formatting | bytes 524288

commit v3 on v2

--- a/solution.py
+++ b/solution.py
@@ -72,7 +72,12 @@
     codes_out,
     codes_in,
     table,
-    tiles,
+    halves,
+    tiles_0,
+    tiles_1,
+    tiles_2,
+    tiles_3,
+    tiles_4,
     sum_blocks,
     sum_children,
     leaf_acc,
@@ -154,30 +159,6 @@
     loads[0].wait()
     for c in range(clusters):
         window[HOPS * clusters + c] = signal_ref[:, c * leaf : (c + 1) * leaf]
-    loads[1].wait()
-    loads[2].wait()
-
-    upper = jnp.zeros((rhs, 128), F32)
-    for p in range(4):
-        packed = jnp.zeros((rhs, 128), F32)
-        lifted = [jnp.zeros((rhs, 128), F32) for _ in range(8)]
-        for b in range(4):
-            c = p * 4 + b
-            columns = slice(c * leaf, (c + 1) * leaf)
-            shape = basis_ref[:, columns]
-            moment = lax.dot_general(
-                signal_ref[:, columns],
-                jnp.concatenate([shape] * 4, axis=0),
-                NT,
-                preferred_element_type=F32,
-            )
-            packed = jnp.where(group == b, moment, packed)
-            lift = transfer_ref[c : c + 1, :]
-            lifted = [a + moment * lift[:, g * 128 : (g + 1) * 128] for g, a in enumerate(lifted)]
-        table[x, z, y, core, p] = encode(packed)
-        total = dot_two(jnp.concatenate(lifted, axis=1), sum_blocks[...])
-        upper = jnp.where(group == p, total, upper)
-    table[x, z, y, core, 4] = encode(upper)
 
     pl.semaphore_wait(barrier, len(peers))
 
@@ -214,34 +195,65 @@
     def sig(src, dst, index, device):
         return start(remote(place(src), place(dst), sig_send.at[index], sig_recv.at[index], device))
 
+    def moments():
+        loads[1].wait()
+        loads[2].wait()
+        upper = jnp.zeros((rhs, 128), F32)
+        for p in range(4):
+            packed = jnp.zeros((rhs, 128), F32)
+            lifted = [jnp.zeros((rhs, 128), F32) for _ in range(8)]
+            for b in range(4):
+                c = p * 4 + b
+                columns = slice(c * leaf, (c + 1) * leaf)
+                shape = basis_ref[:, columns]
+                moment = lax.dot_general(
+                    signal_ref[:, columns],
+                    jnp.concatenate([shape] * 4, axis=0),
+                    NT,
+                    preferred_element_type=F32,
+                )
+                packed = jnp.where(group == b, moment, packed)
+                lift = transfer_ref[c : c + 1, :]
+                lifted = [a + moment * lift[:, g * 128 : (g + 1) * 128] for g, a in enumerate(lifted)]
+            table[x, z, y, core, p] = encode(packed)
+            total = dot_two(jnp.concatenate(lifted, axis=1), sum_blocks[...])
+            upper = jnp.where(group == p, total, upper)
+        table[x, z, y, core, 4] = encode(upper)
+
+    lower, upper_half = pl.ds(0, 2), pl.ds(2, 2)
+
     def rows_along_y():
         own = table.at[x, z, y, core]
         return [tab(own, i, peer) for i, peer in enumerate(y_peers)]
 
-    def rows_out(copies):
+    def halves_out(copies):
         arrived(copies)
-        row = table.at[x, z, :, core]
-        return [tab(row, 3 + i, peer) for i, peer in enumerate(x_peers)] + [
-            tab(row, 6 + i, peer) for i, peer in enumerate(z_peers)
-        ]
-
-    def halves_out(copies):
-        more = []
+        a = table.at[x, z, lower, core]
+        b = table.at[x, z, upper_half, core]
+        first = [tab(a, 3 + i, peer) for i, peer in enumerate(x_peers)]
+        first += [tab(b, 6 + i, peer) for i, peer in enumerate(z_peers)]
+        second = [tab(a, 9 + i, peer) for i, peer in enumerate(z_peers)]
+        second += [tab(b, 12 + i, peer) for i, peer in enumerate(x_peers)]
+        return first, second
+
+    def halves_on(first, second):
+        along_z, along_x = [], []
         for i, step in enumerate(steps):
-            copies[i].wait_recv()
-            half = table.at[turn(x, -step), z, pl.ds(0, 2), core]
-            more += [tab(half, 9 + 3 * i + j, peer) for j, peer in enumerate(z_peers)]
-            copies[3 + i].wait_recv()
-            half = table.at[x, turn(z, -step), pl.ds(2, 2), core]
-            more += [tab(half, 18 + 3 * i + j, peer) for j, peer in enumerate(x_peers)]
-        return more + [par(table.at[:, z, :, core], 0)]
-
-    def to_other_core(copies):
+            first[i].wait_recv()
+            half = table.at[turn(x, -step), z, lower, core]
+            along_z.append([tab(half, 15 + 3 * i + j, peer) for j, peer in enumerate(z_peers)])
+            first[3 + i].wait_recv()
+            half = table.at[x, turn(z, -step), upper_half, core]
+            along_x.append([tab(half, 24 + 3 * i + j, peer) for j, peer in enumerate(x_peers)])
+        return along_z, along_x, second
+
+    def to_other_core(along_z, along_x, second):
+        arrived(second[3:])
+        copies = [par(table.at[:, z, :, core], 0)]
         for j, step in enumerate(steps):
-            arrived([copies[6 * i + j] for i in range(3)])
-            arrived([copies[6 * j + 3 + i] for i in range(3)])
+            arrived([second[j]] + [row[j] for row in along_z] + along_x[j])
             copies.append(par(table.at[:, turn(z, -step), :, core], 1 + j))
-        return copies[18:]
+        return copies
 
     window_row = lax.broadcasted_iota(jnp.int32, (1, 256), 1)
 
@@ -250,11 +262,9 @@
         return jnp.minimum(offset, OFFS - 1) * clusters + slot_ref[k, c]
 
     def outward(first, count):
-        for copy in near_in[first : first + count]:
-            copy.wait()
-
         @pl.loop(first, first + count)
         def _(c):
+            pltpu.make_async_copy(near_hbm.at[c], near_buf.at[c], near_sem.at[c]).wait()
             here = signal_ref[:, pl.ds(pl.multiple_of(c * leaf, leaf), leaf)]
             for k in range(near):
                 rows = pl.ds(pl.multiple_of((c * near + k) * rhs, rhs), rhs)
@@ -341,56 +351,77 @@
                 )
             out_ref[:, pl.ds(pl.multiple_of(c * leaf, leaf), leaf)] = total
 
-    def picked(device, block, quarter):
-        tile = table[device >> 5, (device >> 3) & 3, (device >> 1) & 3, device & 1, block]
-        level = tile.astype(jnp.int32).astype(F32)
-        return split(decode(jnp.where(group == quarter, level, 0.0)))
-
-    def coupled(buf, row, pick):
+    def decode_plane(pz, pcore):
+        @pl.loop(0, 16)
+        def _(i):
+            px, py = i // 4, i % 4
+            for block in range(5):
+                level = table[px, pz, py, pcore, block].astype(jnp.int32).astype(F32)
+                high, low = split(decode(level))
+                halves[(px * 32 + pz * 8 + py * 2 + pcore) * 5 + block] = jnp.concatenate(
+                    [high, low], axis=1
+                )
+
+    pair_group = lax.broadcasted_iota(jnp.int32, (rhs, 256), 1) // 32 % 4
+
+    def fetch(pick, tiles):
         for first in (0, 16):
-            pairs = [pick(first + k) for k in range(16)]
-            both = jnp.concatenate(
-                [jnp.concatenate([pair[i] for pair in pairs], axis=0) for i in range(2)], axis=1
-            )
+            picked = []
+            for k in range(first, first + 16):
+                tile, quarter = pick(k)
+                both = halves[tile]
+                picked.append(jnp.where(pair_group == quarter, both, jnp.zeros_like(both)))
             tiles[first * rhs : (first + 16) * rhs, :] = jnp.dot(
-                both, sum_children[:256, :], preferred_element_type=F32
-            )
-
-        def step(eight, sums):
-            factors = buf[row, pl.ds(pl.multiple_of(eight * 8, 8), 8), :]
+                jnp.concatenate(picked, axis=0),
+                sum_children[:256, :],
+                preferred_element_type=F32,
+            )
+
+    def multiply(buf, row, tiles):
+        sums = [jnp.zeros((rhs, 128), F32) for _ in range(8)]
+        for eight in range(4):
+            factors = buf[row, eight * 8 : eight * 8 + 8, :]
             for k in range(8):
-                tile = tiles[pl.ds(pl.multiple_of((eight * 8 + k) * rhs, rhs), rhs), :]
-                sums = tuple(
+                first = (eight * 8 + k) * rhs
+                tile = tiles[first : first + rhs, :]
+                sums = [
                     a + tile * factors[k : k + 1, g * 128 : (g + 1) * 128]
                     for g, a in enumerate(sums)
-                )
-            return sums
-
-        sums = lax.fori_loop(0, 4, step, tuple(jnp.zeros((rhs, 128), F32) for _ in range(8)))
+                ]
         return jnp.concatenate(sums, axis=1)
 
-    def far(first, count):
-        @pl.loop(first, first + count)
+    def top_of(p):
+        def pick(k):
+            j = far_top_ref[p, k]
+            return (j >> 2) * 5 + 4, j & 3
+
+        return pick
+
+    def leaf_of(c):
+        def pick(k):
+            j = far_leaf_ref[c, k]
+            return (j >> 2) + (j >> 4), j & 3
+
+        return pick
+
+    def far():
+        buffers = (tiles_0, tiles_1, tiles_2, tiles_3, tiles_4)
+        fetch(top_of(0), buffers[0])
+
+        @pl.loop(0, 4)
         def _(p):
-            def pick_top(k):
-                j = far_top_ref[p, k]
-                return picked(j >> 2, 4, j & 3)
-
-            top = dot_two(coupled(top_buf, p, pick_top), sum_blocks[...])[:, :32]
+            fetch(leaf_of(p * 4), buffers[1])
+            top = dot_two(multiply(top_buf, p, buffers[0]), sum_blocks[...])[:, :32]
             spread = dot_two(top, sum_blocks[:, :32], NT)
-
-            @pl.loop(0, 4)
-            def _(b):
+            for b in range(4):
                 c = p * 4 + b
-
-                def pick_leaf(k):
-                    j = far_leaf_ref[c, k]
-                    return picked(j >> 4, (j >> 2) & 3, j & 3)
-
-                rows = pl.ds(pl.multiple_of(b * rhs, rhs), rhs)
-                leaf_acc[rows, :] = coupled(leaf_buf, c, pick_leaf)
+                if b < 3:
+                    fetch(leaf_of(c + 1), buffers[b + 2])
+                else:
+                    fetch(top_of(jnp.minimum(p + 1, 3)), buffers[0])
+                rows = slice(b * rhs, (b + 1) * rhs)
+                leaf_acc[rows, :] = multiply(leaf_buf, c, buffers[b + 1])
                 down_acc[rows, :] = spread * transfer_ref[pl.ds(c, 1), :]
-
             field = dot_two(leaf_acc[...], sum_blocks[...]) + dot_two(
                 down_acc[...], sum_children[...]
             )
@@ -401,41 +432,45 @@
                     field[b * rhs : (b + 1) * rhs], basis_ref[:, columns], preferred_element_type=F32
                 )
 
-    legs = rows_along_y()
     signals = [
-        sig(4, 8, 0, surf_peers[0]),
-        sig(4, 6, 1, surf_peers[1]),
-        sig(4, 2, 2, surf_peers[2]),
+        sig(4, 6, 0, surf_peers[1]),
+        sig(4, 2, 1, surf_peers[2]),
+        sig(4, 8, 2, surf_peers[0]),
         sig(4, 0, 3, surf_peers[3]),
     ]
     pairs = [sig(4, 3 + 2 * core, 4, partner)]
+    moments()
+    legs = rows_along_y()
     for copy in loads[3:6]:
         copy.wait()
-    outward(0, 5)
-    legs = rows_out(legs)
-    outward(5, 11)
+    outward(0, 16)
+    legs = halves_out(legs)
     flipped = hot_rows[...].T.astype(BF16)
     hot[...] = jnp.concatenate([flipped, flipped], axis=1)[: OFFS * clusters, :]
     scatter(0)
     stage = [to_partner(0)]
+    arrived(signals[:2])
+    pairs += [sig(2, 1 + 2 * core, 5, partner), sig(6, 5 + 2 * core, 6, partner)]
     scatter(1)
     stage.append(to_partner(1))
-    legs = halves_out(legs)
-    arrived(signals)
-    pairs += [
-        sig(2, 1 + 2 * core, 5, partner),
-        sig(6, 5 + 2 * core, 6, partner),
-        sig(8 - 8 * core, 7 - 6 * core, 7, partner),
-    ]
+    arrived(signals[2:])
+    pairs.append(sig(8 - 8 * core, 7 - 6 * core, 7, partner))
+    legs = halves_on(*legs)
     stage = [to_targets(half, copy) for half, copy in enumerate(stage)]
+    for copy in loads[6:]:
+        copy.wait()
     arrived(pairs)
     inward(0, 12)
-    legs = to_other_core(legs)
+    legs = to_other_core(*legs)
     inward(12, 4)
-    for copy in loads[6:]:
-        copy.wait()
-    arrived(legs)
-    far(0, 4)
+    for step in (0,) + steps:
+        decode_plane(turn(z, -step), core)
+    legs[0].wait_recv()
+    decode_plane(z, 1 - core)
+    for step, copy in zip(steps, legs[1:]):
+        copy.wait_recv()
+        decode_plane(turn(z, -step), 1 - core)
+    far()
     for half, copies in enumerate(stage):
         add_returned(half, copies)
 
@@ -492,6 +527,11 @@
             pltpu.VMEM((4, 2, 272, 128), jnp.int16),
             pltpu.VMEM((4, 2, 272, 128), jnp.int16),
             pltpu.VMEM((4, 4, 4, 2, 5, 16, 128), jnp.int16),
+            pltpu.VMEM((640, 16, 256), BF16),
+            pltpu.VMEM((512, 128), F32),
+            pltpu.VMEM((512, 128), F32),
+            pltpu.VMEM((512, 128), F32),
+            pltpu.VMEM((512, 128), F32),
             pltpu.VMEM((512, 128), F32),
             pltpu.VMEM((1024, 128), BF16),
             pltpu.VMEM((1024, 128), BF16),
@@ -503,8 +543,8 @@
             dma((8,)),
             dma((10,)),
             dma((10,)),
-            dma((27,)),
-            dma((27,)),
+            dma((33,)),
+            dma((33,)),
             dma((4,)),
             dma((4,)),
         ],

time: 55.3 us -> 49.2 us (0.89)
  the two profiles are of different devices: /device:TPU:1 before, /device:TPU:120 now
where the time goes in v3:
time: 49.2 us; the launch traced here: 49.1 us
  Pallas kernels  47.4 us (96%)
  local copies, waits for them, and re-layouts  1.67 us (3%)
    pallas_call x1, Pallas kernels, shards(): pl.pallas_call(kernel, out_shape=jax.ShapeDtypeStruct((16, 4096), F32), i...  47.4 us
    unnamed x1, local copies, waits for them, and re-layouts  1.67 us

profile of v3, /device:TPU:120, one launch (start us, length us, event | category | flops | bytes accessed | tf_op | source)
XLA Modules:
  0.0 49.1 jit_solution(6401387734018530216)
XLA Ops:
  0.0 47.4 %shard_map.109 = f32[16,4096]{1,0:T(8,128)} custom-call(s32[8,16]{1,0:T(8,128)} %bitcast.3, s32[8,16]{1,0:T(8,128)} %bitcast.4, s32[8,16]{1,0:T(8,128)} %bitcast.5, s32[16,32]{1,0:T(8,128)} %far_leaf_hbm.1, s32[4,32]{1,0:T(4,128)} %far_top_hbm.1, bf16[16,4096]{1,0:T(8,128)(2,1)} %signal_hbm.1, bf16[32,4096]{1,0:T(8,128)(2,1)} %basis_hbm.1, ...), custom_call_target="tpu_custom_call" | custom-call | flops 1200000000 | bytes 20000000 | tf_op jit(solution)/shard_map/pallas_call | solution.py:503
  47.4 1.7 %copy.13 = f32[16,4096]{1,0:T(8,128)} copy(f32[16,4096]{1,0:T(8,128)} %shard_map.109) | data formatting | bytes 524288

commit v4 on v3

--- a/solution.py
+++ b/solution.py
@@ -380,12 +380,11 @@
     def multiply(buf, row, tiles):
         sums = [jnp.zeros((rhs, 128), F32) for _ in range(8)]
         for eight in range(4):
-            factors = buf[row, eight * 8 : eight * 8 + 8, :]
             for k in range(8):
                 first = (eight * 8 + k) * rhs
                 tile = tiles[first : first + rhs, :]
                 sums = [
-                    a + tile * factors[k : k + 1, g * 128 : (g + 1) * 128]
+                    a + tile * buf[row, eight * 8 + k : eight * 8 + k + 1, g * 128 : (g + 1) * 128]
                     for g, a in enumerate(sums)
                 ]
         return jnp.concatenate(sums, axis=1)
@@ -456,11 +455,11 @@
     arrived(signals[2:])
     pairs.append(sig(8 - 8 * core, 7 - 6 * core, 7, partner))
     legs = halves_on(*legs)
-    stage = [to_targets(half, copy) for half, copy in enumerate(stage)]
     for copy in loads[6:]:
         copy.wait()
     arrived(pairs)
     inward(0, 12)
+    stage = [to_targets(half, copy) for half, copy in enumerate(stage)]
     legs = to_other_core(*legs)
     inward(12, 4)
     for step in (0,) + steps:

time: 49.2 us -> 47.9 us (0.974)
  the two profiles are of different devices: /device:TPU:120 before, /device:TPU:1 now
where the time goes in v4:
time: 47.9 us; the launch traced here: 47.3 us
  Pallas kernels  45.6 us (95%)
  local copies, waits for them, and re-layouts  1.67 us (3%)
    pallas_call x1, Pallas kernels, shards(): pl.pallas_call(kernel, out_shape=jax.ShapeDtypeStruct((16, 4096), F32), i...  45.6 us
    unnamed x1, local copies, waits for them, and re-layouts  1.67 us

profile of v4, /device:TPU:1, one launch (start us, length us, event | category | flops | bytes accessed | tf_op | source)
XLA Modules:
  0.0 47.3 jit_solution(506619886341767170)
XLA Ops:
  0.0 45.6 %shard_map.109 = f32[16,4096]{1,0:T(8,128)} custom-call(s32[8,16]{1,0:T(8,128)} %bitcast.3, s32[8,16]{1,0:T(8,128)} %bitcast.4, s32[8,16]{1,0:T(8,128)} %bitcast.5, s32[16,32]{1,0:T(8,128)} %far_leaf_hbm.1, s32[4,32]{1,0:T(4,128)} %far_top_hbm.1, bf16[16,4096]{1,0:T(8,128)(2,1)} %signal_hbm.1, bf16[32,4096]{1,0:T(8,128)(2,1)} %basis_hbm.1, ...), custom_call_target="tpu_custom_call" | custom-call | flops 1200000000 | bytes 20000000 | tf_op jit(solution)/shard_map/pallas_call | solution.py:502
  45.6 1.7 %copy.13 = f32[16,4096]{1,0:T(8,128)} copy(f32[16,4096]{1,0:T(8,128)} %shard_map.109) | data formatting | bytes 524288
